TPU v7x, 32 devices: a whole 2x2x4 slice. The times are simulated.
32 devices in a mesh: seq: 16 (over z, x, core), fsdp: 2 (over y).
Axes of the slice: x: 2, y: 2, z: 4, core: 2. Of those that a mesh axis runs over, the one named last changes fastest.
Arguments:
- text_states: bfloat16 [4096, 8192], P('seq'), may hold values from -6 to 6
- images: bfloat16 [16, 1601, 8192], P('seq', None, 'fsdp'), may hold values from -6 to 6
- norm_gain: float32 [8192], replicated, may hold values from 0.1 to 1.9
- query_weight: bfloat16 [8192, 4096], P('seq', 'fsdp'), may hold values from -0.0625 to 0.0625
- image_projection_weight: bfloat16 [8192, 2048], P(('fsdp', 'seq')), may hold values from -0.0625 to 0.0625
- query_gain: float32 [128], replicated, may hold values from 0.5 to 2
- key_gain: float32 [128], replicated, may hold values from 0.5 to 2
- admission: int32 [16, 16], P('seq'), may hold values from 0 to 1, as said below
Outputs:
- attended: bfloat16 [4096, 4096], P('seq', 'fsdp')
Inputs may be any that keep to these rules, and one draw needn't show every extreme that they name: admission[c, m] is 1 for m = c and for at most 2 of the images m with c - 4 <= m < c, and 0 elsewhere; in every draw some text blocks, the last one among them, attend to exactly 3 images.
All inputs are finite; a program needn't handle non-finite values.
Results may differ from a plain program's by a relative error of at most 0.035.
Values may be sent and summed in bfloat16 or wider, within the bound.
A program may use at most 128 MiB of HBM per device.

v0:
```python
import math

import jax
import jax.numpy as jnp
from jax import lax
from jax.sharding import PartitionSpec as P

KEY_VALUE_HEADS = 8
IMAGE_LOOKBACK = 4


def from_behind(value, axis, steps):
    count = lax.axis_size(axis)
    initial, last = (max(0, -steps), min(count, count - steps))
    return lax.ppermute(value, axis, [(source, source + steps) for source in range(initial, last)])


def rms_scale(values, gain):
    return values * lax.rsqrt(jnp.mean(values * values, axis=-1, keepdims=True) + 1e-05) * gain


def attend(query_heads, stacked, admitted):
    slot_count, kv_heads, image_tokens, double_width = stacked.shape
    head_dim = double_width // 2
    row_count, heads_local, _ = query_heads.shape
    heads_per_group = heads_local // kv_heads
    grouped = query_heads.reshape(row_count, kv_heads, heads_per_group, head_dim)
    grouped = grouped.transpose(1, 2, 0, 3).reshape(kv_heads, heads_per_group * row_count, head_dim)
    per_head = jnp.moveaxis(stacked, 1, 0).reshape(
        kv_heads, slot_count * image_tokens, double_width
    )
    column_live = jnp.repeat(admitted, image_tokens)
    score_scale = 1.0 / math.sqrt(head_dim)

    def one_head(operands):
        query_rows, key_value_pair = operands
        scores = (
            lax.dot_general(
                query_rows,
                key_value_pair[:, :head_dim],
                (((1,), (1,)), ((), ())),
                preferred_element_type=jnp.float32,
            )
            * score_scale
        )
        scores = jnp.where(column_live[None, :], scores, -jnp.inf)
        row_peak = jnp.max(scores, axis=1, keepdims=True)
        weights = jnp.exp(scores - row_peak)
        row_total = jnp.sum(weights, axis=1, keepdims=True)
        blended = jnp.dot(
            weights.astype(jnp.bfloat16),
            key_value_pair[:, head_dim:],
            preferred_element_type=jnp.float32,
        )
        return blended / row_total

    outputs = lax.map(one_head, (grouped, per_head))
    outputs = outputs.reshape(kv_heads, heads_per_group, row_count, head_dim).transpose(2, 0, 1, 3)
    return outputs.reshape(row_count, heads_local * head_dim).astype(jnp.bfloat16)


def on_device(
    text_states,
    images,
    norm_gain,
    query_weight,
    image_projection_weight,
    query_gain,
    key_gain,
    admission,
):
    head_dim = query_gain.shape[0]
    local_key_value = KEY_VALUE_HEADS // lax.axis_size("fsdp")
    heads_local = query_weight.shape[1] // head_dim
    row_count = text_states.shape[0]
    normed = rms_scale(text_states.astype(jnp.float32), norm_gain).astype(jnp.bfloat16)
    columns = normed
    queries = jnp.dot(
        columns,
        lax.all_gather(query_weight, "seq", axis=0, tiled=True),
        preferred_element_type=jnp.float32,
    )
    query_heads = rms_scale(queries.reshape(row_count, heads_local, head_dim), query_gain).astype(
        jnp.bfloat16
    )
    weight_block = lax.all_gather(image_projection_weight, "seq", axis=0, tiled=True)
    features = images[0]
    columns = weight_block
    score_product = jnp.dot(features, columns, preferred_element_type=jnp.float32)
    own_kv = lax.psum_scatter(
        score_product.reshape(
            features.shape[0], local_key_value * lax.axis_size("fsdp"), 2 * head_dim
        )
        .transpose(1, 0, 2)
        .astype(jnp.bfloat16),
        "fsdp",
        scatter_dimension=0,
        tiled=True,
    ).astype(jnp.float32)
    key_part = rms_scale(own_kv[..., :head_dim], key_gain)
    packed = jnp.concatenate([key_part, own_kv[..., head_dim:]], axis=-1).astype(jnp.bfloat16)
    image_window = [packed]
    for distance in range(1, IMAGE_LOOKBACK + 1):
        image_window.append(from_behind(packed, "seq", distance))
    stacked = jnp.stack(image_window)
    span_index = lax.axis_index("seq")
    image_ids = span_index - jnp.arange(IMAGE_LOOKBACK + 1, dtype=jnp.int32)
    admitted = (image_ids >= 0) & (jnp.take(admission[0], jnp.maximum(image_ids, 0)) == 1)
    return attend(query_heads, stacked, admitted)


def solution(mesh):
    placed = (
        P("seq", None),
        P("seq", None, "fsdp"),
        P(),
        P("seq", "fsdp"),
        P(("fsdp", "seq"), None),
        P(),
        P(),
        P("seq", None),
    )
    return jax.shard_map(
        on_device, mesh=mesh, in_specs=placed, out_specs=P("seq", "fsdp"), check_vma=False
    )
```

profile of v0, /device:TPU:27, one launch (start us, length us, event | category | flops | bytes accessed | tf_op | source)
XLA Modules:
  0.0 950.4 jit_solution(12120618289018594295)
XLA Ops:
  7.3 127.6 %all-gather.5.cloned.1.call-done = bf16[4096,2048]{1,0:T(8,128)(2,1)} async-done(((bf16[256,2048]{1,0:T(8,128)(2,1)}), bf16[4096,2048]{1,0:T(8,128)(2,1)}) %all-gather.5.cloned.1.call-update) | async-done | bytes 16777232 | tf_op jit(solution)/shard_map/all_gather | solution.py:86
  134.9 20.8 %copy.34 = bf16[2048,4096]{1,0:T(8,128)(2,1)} copy(bf16[2048,4096]{0,1:T(8,128)(2,1)} %bitcast.59) | data formatting | bytes 33554432 | tf_op jit(solution)/shard_map/dot_general | solution.py:89
  155.6 35.5 %convert_bitcast_fusion = bf16[8,1601,256]{2,1,0:T(8,128)(2,1)} fusion(bf16[8,256,4096]{2,1,0:T(8,128)(2,1)} %bitcast.60, bf16[1,1601,4096]{2,1,0:T(8,128)(2,1)} %param.11), kind=kOutput, calls=%fused_computation.28 | convolution fusion | flops 26863601664 | bytes 36450304 | tf_op jit(solution)/shard_map/dot_general | solution.py:89
  191.9 80.4 %reduce-scatter.2.cloned.1.call-done = bf16[4,1601,256]{2,1,0:T(8,128)(2,1)} async-done(((bf16[8,1601,256]{2,1,0:T(8,128)(2,1)}), bf16[4,1601,256]{2,1,0:T(8,128)(2,1)}) %reduce-scatter.2.cloned.1.call-update) | async-done | bytes 3278864 | tf_op jit(solution)/shard_map/reduce_scatter | solution.py:90
  277.8 9.9 %copy.35 = bf16[4,1601,256]{2,0,1:T(4,128)(2,1)} copy(bf16[4,1601,256]{2,1,0:T(8,128)(2,1)S(1)} %pad_maximum_fusion) | data formatting | bytes 6557696 | tf_op jit(solution)/shard_map/concatenate | solution.py:101
  302.4 270.9 %collective-permute-done.1 = bf16[4,1601,256]{2,0,1:T(4,128)(2,1)} collective-permute-done((bf16[4,1601,256]{2,0,1:T(4,128)(2,1)}, bf16[4,1601,256]{2,0,1:T(4,128)(2,1)}, u32[]{:S(2)}, u32[]{:S(2)}) %collective-permute-start.1) | collective-permute-done | bytes 3278880 | tf_op jit(solution)/shard_map/ppermute | solution.py:15
  578.2 106.6 %collective-permute-done.3 = bf16[4,1601,256]{2,0,1:T(4,128)(2,1)S(1)} collective-permute-done((bf16[4,1601,256]{2,0,1:T(4,128)(2,1)}, bf16[4,1601,256]{2,0,1:T(4,128)(2,1)S(1)}, u32[]{:S(2)}, u32[]{:S(2)}) %collective-permute-start.3) | collective-permute-done | bytes 3278880 | tf_op jit(solution)/shard_map/ppermute | solution.py:15
  685.2 7.5 copy.43
  692.7 12.7 %reshape.104 = bf16[4,8005,256]{2,1,0:T(8,128)(2,1)} reshape(bf16[4,5,1601,256]{3,2,1,0:T(8,128)(2,1)} %copy.43) | data formatting | bytes 32788480 | tf_op jit(solution)/shard_map/reshape | solution.py:29
  705.4 16.3 %fusion.38 = f32[256,2048]{1,0:T(8,128)S(1)} fusion(bf16[8192,2048]{1,0:T(8,128)(2,1)} %all-gather.3.cloned.1.call-done, bf16[256,8192]{1,0:T(8,128)(2,1)} %param.10, f32[8192]{0:T(1024)S(1)} %copy-done.10, f32[256]{0:T(256)S(1)} %add_rsqrt_fusion.2), kind=kOutput, calls=%fused_computation.29 | convolution fusion | flops 8598323200 | bytes 39879680 | tf_op jit(solution)/shard_map/dot_general | solution.py:78
  735.0 205.2 %while.11 = (s32[]{:T(128)}, bf16[4,1024,128]{2,1,0:T(8,128)(2,1)}, bf16[4,1024,128]{2,1,0:T(8,128)(2,1)S(1)}, bf16[4,8005,256]{2,1,0:T(8,128)(2,1)}, pred[5]{0:T(512)(128)(4,1)S(1)}, /*index=5*/s32[]{:T(128)}) while((s32[]{:T(128)}, bf16[4,1024,128]{2,1,0:T(8,128)(2,1)}, bf16[4,1024,128]{2,1,0:T(8,128)(2,1)S(1)}, ...), condition=%wide.region_7.8_spmd.clone, body=%wide.region_4.7_spmd.clone.sunk | while | flops 4287222784 | bytes 136301504 | solution.py:57
  735.2 4.4 dynamic-slice_bitcast_fusion.2
  739.8 13.8 %fusion.53 = (f32[1024]{0:T(1024)S(1)}, f32[1024,8005]{0,1:T(8,128)}) fusion(pred[8005]{0:T(1024)(128)(4,1)S(1)} %broadcast_in_dim.81, bf16[8005,256]{1,0:T(8,128)(2,1)} %dynamic-slice_bitcast_fusion.2, bf16[4,1024,128]{2,1,0:T(8,128)(2,1)S(1)} %get-tuple-element.107, s32[]{:T(128)} %get-tuple-element.99), kind=kOutput, calls=%fused_computation.4.clone.1 | convolution fusion | flops 2123053056 | bytes 35113472 | tf_op jit(solution)/shard_map/while/body/eval_jaxpr/dot_general | solution.py:38
  753.6 15.3 %fusion.54 = f32[1024]{0:T(1024)S(1)} fusion(f32[1024,8005]{0,1:T(8,128)} %get-tuple-element.91, f32[1024]{0:T(1024)S(1)} %get-tuple-element.92, pred[8005]{0:T(1024)(128)(4,1)S(1)} %broadcast_in_dim.81), kind=kLoop, calls=%fused_computation.5.clone.1 | loop fusion | flops 32787456 | bytes 32804676 | tf_op jit(solution)/shard_map/while/body/eval_jaxpr/reduce_sum | solution.py:49
  769.0 16.5 %fusion.55 = bf16[4,1024,128]{2,1,0:T(8,128)(2,1)S(1)} fusion(bf16[4,1024,128]{2,1,0:T(8,128)(2,1)S(1)} %copy-done.6, s32[]{:T(128)} %get-tuple-element.99, bf16[8005,256]{1,0:T(8,128)(2,1)S(1)} %copy-done.2, f32[1024,8005]{0,1:T(8,128)} %get-tuple-element.91, f32[1024]{0:T(1024)S(1)} %get-tuple-element.92, ...), kind=kOutput, calls=%fused_computation.15.clone.1 | convolution fusion | flops 2131382272 | bytes 35379204 | tf_op jit(solution)/shard_map/while/body/eval_jaxpr/dot_general | solution.py:50
  791.0 13.9 %fusion.53 = (f32[1024]{0:T(1024)S(1)}, f32[1024,8005]{0,1:T(8,128)}) fusion(pred[8005]{0:T(1024)(128)(4,1)S(1)} %broadcast_in_dim.81, bf16[8005,256]{1,0:T(8,128)(2,1)} %dynamic-slice_bitcast_fusion.2, bf16[4,1024,128]{2,1,0:T(8,128)(2,1)S(1)} %get-tuple-element.107, s32[]{:T(128)} %get-tuple-element.99), kind=kOutput, calls=%fused_computation.4.clone.1 | convolution fusion | flops 2123053056 | bytes 35113472 | tf_op jit(solution)/shard_map/while/body/eval_jaxpr/dot_general | solution.py:38
  804.9 15.3 %fusion.54 = f32[1024]{0:T(1024)S(1)} fusion(f32[1024,8005]{0,1:T(8,128)} %get-tuple-element.91, f32[1024]{0:T(1024)S(1)} %get-tuple-element.92, pred[8005]{0:T(1024)(128)(4,1)S(1)} %broadcast_in_dim.81), kind=kLoop, calls=%fused_computation.5.clone.1 | loop fusion | flops 32787456 | bytes 32804676 | tf_op jit(solution)/shard_map/while/body/eval_jaxpr/reduce_sum | solution.py:49
  820.2 16.5 %fusion.55 = bf16[4,1024,128]{2,1,0:T(8,128)(2,1)S(1)} fusion(bf16[4,1024,128]{2,1,0:T(8,128)(2,1)S(1)} %copy-done.6, s32[]{:T(128)} %get-tuple-element.99, bf16[8005,256]{1,0:T(8,128)(2,1)S(1)} %copy-done.2, f32[1024,8005]{0,1:T(8,128)} %get-tuple-element.91, f32[1024]{0:T(1024)S(1)} %get-tuple-element.92, ...), kind=kOutput, calls=%fused_computation.15.clone.1 | convolution fusion | flops 2131382272 | bytes 35379204 | tf_op jit(solution)/shard_map/while/body/eval_jaxpr/dot_general | solution.py:50
  842.2 13.9 %fusion.53 = (f32[1024]{0:T(1024)S(1)}, f32[1024,8005]{0,1:T(8,128)}) fusion(pred[8005]{0:T(1024)(128)(4,1)S(1)} %broadcast_in_dim.81, bf16[8005,256]{1,0:T(8,128)(2,1)} %dynamic-slice_bitcast_fusion.2, bf16[4,1024,128]{2,1,0:T(8,128)(2,1)S(1)} %get-tuple-element.107, s32[]{:T(128)} %get-tuple-element.99), kind=kOutput, calls=%fused_computation.4.clone.1 | convolution fusion | flops 2123053056 | bytes 35113472 | tf_op jit(solution)/shard_map/while/body/eval_jaxpr/dot_general | solution.py:38
  856.1 15.3 %fusion.54 = f32[1024]{0:T(1024)S(1)} fusion(f32[1024,8005]{0,1:T(8,128)} %get-tuple-element.91, f32[1024]{0:T(1024)S(1)} %get-tuple-element.92, pred[8005]{0:T(1024)(128)(4,1)S(1)} %broadcast_in_dim.81), kind=kLoop, calls=%fused_computation.5.clone.1 | loop fusion | flops 32787456 | bytes 32804676 | tf_op jit(solution)/shard_map/while/body/eval_jaxpr/reduce_sum | solution.py:49
  871.5 16.5 %fusion.55 = bf16[4,1024,128]{2,1,0:T(8,128)(2,1)S(1)} fusion(bf16[4,1024,128]{2,1,0:T(8,128)(2,1)S(1)} %copy-done.6, s32[]{:T(128)} %get-tuple-element.99, bf16[8005,256]{1,0:T(8,128)(2,1)S(1)} %copy-done.2, f32[1024,8005]{0,1:T(8,128)} %get-tuple-element.91, f32[1024]{0:T(1024)S(1)} %get-tuple-element.92, ...), kind=kOutput, calls=%fused_computation.15.clone.1 | convolution fusion | flops 2131382272 | bytes 35379204 | tf_op jit(solution)/shard_map/while/body/eval_jaxpr/dot_general | solution.py:50
  893.5 13.9 %fusion.53 = (f32[1024]{0:T(1024)S(1)}, f32[1024,8005]{0,1:T(8,128)}) fusion(pred[8005]{0:T(1024)(128)(4,1)S(1)} %broadcast_in_dim.81, bf16[8005,256]{1,0:T(8,128)(2,1)} %dynamic-slice_bitcast_fusion.2, bf16[4,1024,128]{2,1,0:T(8,128)(2,1)S(1)} %get-tuple-element.107, s32[]{:T(128)} %get-tuple-element.99), kind=kOutput, calls=%fused_computation.4.clone.1 | convolution fusion | flops 2123053056 | bytes 35113472 | tf_op jit(solution)/shard_map/while/body/eval_jaxpr/dot_general | solution.py:38
  907.3 15.3 %fusion.54 = f32[1024]{0:T(1024)S(1)} fusion(f32[1024,8005]{0,1:T(8,128)} %get-tuple-element.91, f32[1024]{0:T(1024)S(1)} %get-tuple-element.92, pred[8005]{0:T(1024)(128)(4,1)S(1)} %broadcast_in_dim.81), kind=kLoop, calls=%fused_computation.5.clone.1 | loop fusion | flops 32787456 | bytes 32804676 | tf_op jit(solution)/shard_map/while/body/eval_jaxpr/reduce_sum | solution.py:49
  922.7 16.5 %fusion.55 = bf16[4,1024,128]{2,1,0:T(8,128)(2,1)S(1)} fusion(bf16[4,1024,128]{2,1,0:T(8,128)(2,1)S(1)} %copy-done.6, s32[]{:T(128)} %get-tuple-element.99, bf16[8005,256]{1,0:T(8,128)(2,1)S(1)} %copy-done.2, f32[1024,8005]{0,1:T(8,128)} %get-tuple-element.91, f32[1024]{0:T(1024)S(1)} %get-tuple-element.92, ...), kind=kOutput, calls=%fused_computation.15.clone.1 | convolution fusion | flops 2131382272 | bytes 35379204 | tf_op jit(solution)/shard_map/while/body/eval_jaxpr/dot_general | solution.py:50
  (97 shorter events, 61.3 us)
Async XLA Ops:
  6.5 288.2 %copy-start = (s32[1,16]{1,0:T(1,128)S(1)}, s32[1,16]{1,0:T(1,128)}, u32[]{:S(2)}) copy-start(s32[1,16]{1,0:T(1,128)} %param.17) | copy-start | bytes 196
  6.5 128.4 %all-gather.5.cloned.1.call-start = ((), (), s32[]{:S(2)}) async-start(), calls=%async_computation.2 | async-start | bytes 17825792 | tf_op jit(solution)/shard_map/all_gather | solution.py:86
  7.3 265.0 %reduce-scatter.2.cloned.1.call-start = ((), (), s32[]{:S(2)}) async-start(), calls=%async_computation.3 | async-start | bytes 9879552 | tf_op jit(solution)/shard_map/reduce_scatter | solution.py:90
  191.1 514.3 %all-gather.3.cloned.1.call-start = ((), (), s32[]{:S(2)}) async-start(), calls=%async_computation.1 | async-start | bytes 35651584 | tf_op jit(solution)/shard_map/all_gather | solution.py:80
  191.9 83.8 %copy-start.8 = (f32[128]{0:T(128)S(1)}, f32[128]{0:T(128)}, u32[]{:S(2)}) copy-start(f32[128]{0:T(128)} %param.16) | copy-start | bytes 1540
  274.7 3.1 copy-start.3
  274.7 2.7 slice-start
  277.8 19.1 %copy-start.4 = (bf16[4,1601,256]{2,1,0:T(8,128)(2,1)S(1)}, bf16[4,1601,256]{2,1,0:T(8,128)(2,1)}, u32[]{:S(2)}) copy-start(bf16[4,1601,256]{2,1,0:T(8,128)(2,1)} %reduce-scatter.2.cloned.1.call-done) | copy-start | bytes 9836548
  287.7 12.4 %collective-permute-start = (bf16[4,1601,256]{2,0,1:T(4,128)(2,1)}, bf16[4,1601,256]{2,0,1:T(4,128)(2,1)}, u32[]{:S(2)}, u32[]{:S(2)}) collective-permute-start(bf16[4,1601,256]{2,0,1:T(4,128)(2,1)} %copy.35), channel_id=1, source_target_pairs={{0,2},{2,4},{4,6},{6,8},{8,10},{10,12},{12,14},{14,16},{16,18},{18... | collective-permute-start | bytes 9836552 | tf_op jit(solution)/shard_map/ppermute | solution.py:15
  289.0 284.4 %collective-permute-start.1 = (bf16[4,1601,256]{2,0,1:T(4,128)(2,1)}, bf16[4,1601,256]{2,0,1:T(4,128)(2,1)}, u32[]{:S(2)}, u32[]{:S(2)}) collective-permute-start(bf16[4,1601,256]{2,0,1:T(4,128)(2,1)} %copy.35), channel_id=1, source_target_pairs={{0,4},{2,6},{4,8},{6,10},{8,12},{10,14},{12,16},{14,18},{16,20},{1... | collective-permute-start | bytes 9836552 | tf_op jit(solution)/shard_map/ppermute | solution.py:15
  293.4 282.4 %collective-permute-start.2 = (bf16[4,1601,256]{2,0,1:T(4,128)(2,1)}, bf16[4,1601,256]{2,0,1:T(4,128)(2,1)}, u32[]{:S(2)}, u32[]{:S(2)}) collective-permute-start(bf16[4,1601,256]{2,0,1:T(4,128)(2,1)} %copy.35), channel_id=1, source_target_pairs={{0,6},{2,8},{4,10},{6,12},{8,14},{10,16},{12,18},{14,20},{16,22},{... | collective-permute-start | bytes 9836552 | tf_op jit(solution)/shard_map/ppermute | solution.py:15
  295.4 389.4 %collective-permute-start.3 = (bf16[4,1601,256]{2,0,1:T(4,128)(2,1)}, bf16[4,1601,256]{2,0,1:T(4,128)(2,1)S(1)}, u32[]{:S(2)}, u32[]{:S(2)}) collective-permute-start(bf16[4,1601,256]{2,0,1:T(4,128)(2,1)} %copy.35), channel_id=1, source_target_pairs={{0,8},{2,10},{4,12},{6,14},{8,16},{10,18},{12,20},{14,22},{16,24},... | collective-permute-start | bytes 9836552 | tf_op jit(solution)/shard_map/ppermute | solution.py:15
  692.7 12.7 %copy-start.10 = (f32[8192]{0:T(1024)S(1)}, f32[8192]{0:T(1024)}, u32[]{:S(2)}) copy-start(f32[8192]{0:T(1024)} %param.12) | copy-start | bytes 98308
  721.7 1.3 copy-start.5
  724.5 8.6 copy-start.9
  753.6 15.4 %copy-start.2 = (bf16[8005,256]{1,0:T(8,128)(2,1)S(1)}, bf16[8005,256]{1,0:T(8,128)(2,1)}, u32[]{:S(2)}) copy-start(bf16[8005,256]{1,0:T(8,128)(2,1)} %dynamic-slice_bitcast_fusion.2) | copy-start | bytes 12295684 | tf_op jit(solution)/shard_map/while
  753.6 15.4 %copy-start.6 = (bf16[4,1024,128]{2,1,0:T(8,128)(2,1)S(1)}, bf16[4,1024,128]{2,1,0:T(8,128)(2,1)}, u32[]{:S(2)}) copy-start(bf16[4,1024,128]{2,1,0:T(8,128)(2,1)} %get-tuple-element.100) | copy-start | bytes 3145732 | tf_op jit(solution)/shard_map/while
  804.9 15.4 %copy-start.2 = (bf16[8005,256]{1,0:T(8,128)(2,1)S(1)}, bf16[8005,256]{1,0:T(8,128)(2,1)}, u32[]{:S(2)}) copy-start(bf16[8005,256]{1,0:T(8,128)(2,1)} %dynamic-slice_bitcast_fusion.2) | copy-start | bytes 12295684 | tf_op jit(solution)/shard_map/while
  804.9 15.4 %copy-start.6 = (bf16[4,1024,128]{2,1,0:T(8,128)(2,1)S(1)}, bf16[4,1024,128]{2,1,0:T(8,128)(2,1)}, u32[]{:S(2)}) copy-start(bf16[4,1024,128]{2,1,0:T(8,128)(2,1)} %get-tuple-element.100) | copy-start | bytes 3145732 | tf_op jit(solution)/shard_map/while
  856.1 15.4 %copy-start.2 = (bf16[8005,256]{1,0:T(8,128)(2,1)S(1)}, bf16[8005,256]{1,0:T(8,128)(2,1)}, u32[]{:S(2)}) copy-start(bf16[8005,256]{1,0:T(8,128)(2,1)} %dynamic-slice_bitcast_fusion.2) | copy-start | bytes 12295684 | tf_op jit(solution)/shard_map/while
  856.1 15.4 %copy-start.6 = (bf16[4,1024,128]{2,1,0:T(8,128)(2,1)S(1)}, bf16[4,1024,128]{2,1,0:T(8,128)(2,1)}, u32[]{:S(2)}) copy-start(bf16[4,1024,128]{2,1,0:T(8,128)(2,1)} %get-tuple-element.100) | copy-start | bytes 3145732 | tf_op jit(solution)/shard_map/while
  907.3 15.4 %copy-start.2 = (bf16[8005,256]{1,0:T(8,128)(2,1)S(1)}, bf16[8005,256]{1,0:T(8,128)(2,1)}, u32[]{:S(2)}) copy-start(bf16[8005,256]{1,0:T(8,128)(2,1)} %dynamic-slice_bitcast_fusion.2) | copy-start | bytes 12295684 | tf_op jit(solution)/shard_map/while
  907.3 15.4 %copy-start.6 = (bf16[4,1024,128]{2,1,0:T(8,128)(2,1)S(1)}, bf16[4,1024,128]{2,1,0:T(8,128)(2,1)}, u32[]{:S(2)}) copy-start(bf16[4,1024,128]{2,1,0:T(8,128)(2,1)} %get-tuple-element.100) | copy-start | bytes 3145732 | tf_op jit(solution)/shard_map/while
  940.2 3.7 copy-start.1
  (4 other events, 3.9 us)
Sparse Core Ops, SparseCore 0:
  9.5 125.3 all-gather.4
  191.3 80.9 reduce-scatter.1
  273.9 313.0 all-gather.2
where the time goes:
time: 953 us; the launch traced here: 950 us
  waiting for transfers between devices  587 us (62%)
  matrix products  173 us (18%)
  local copies, waits for them, and re-layouts  93.5 us (10%)
  other arithmetic  77.4 us (8%)
  between operations  13.4 us (1%)
    ppermute x4, waiting for transfers between devices, from_behind(): lax.ppermute(value, axis, [(source, source + steps) for source in range(i...  378 us
    all_gather x1, waiting for transfers between devices, on_device(): lax.all_gather(image_projection_weight, 'seq', axis=0, tiled=True)  128 us
    reduce_scatter x1, waiting for transfers between devices, on_device(): lax.psum_scatter(score_product.reshape(features.shape[0], local_key_value...  80.4 us
    dot_general x4, matrix products, one_head(): jnp.dot(weights.astype(jnp.bfloat16), key_value_pair[:, head_dim:], prefe...  66 us
    reduce_sum x4, other arithmetic, one_head(): row_total = jnp.sum(weights, axis=1, keepdims=True)  61.4 us
    dot_general x4, matrix products, one_head(): lax.dot_general(query_rows, key_value_pair[:, :head_dim], (((1,), (1,)),...  55.4 us
    dot_general x1, matrix products, on_device(): jnp.dot(features, columns, preferred_element_type=jnp.float32)  35.5 us
    dot_general x1, local copies, waits for them, and re-layouts, on_device(): jnp.dot(features, columns, preferred_element_type=jnp.float32)  20.8 us
  transfers between devices with their start and end apart: 7, of which 5 were waited for; matrix products, arithmetic and copies ran while one was open for 5% of the time, Pallas kernels for 0%

commit v1 on v0

v1 whole, which is shorter than its diff:
```python
import math

import jax
import jax.numpy as jnp
from jax import lax
from jax.experimental import pallas as pl
from jax.experimental.pallas import tpu as pltpu
from jax.sharding import PartitionSpec as P

KEY_VALUE_HEADS = 8
IMAGE_LOOKBACK = 4
PLANE = 4
EPS = 1e-05


def rms_scale(values, gain):
    return values * lax.rsqrt(jnp.mean(values * values, axis=-1, keepdims=True) + EPS) * gain


def swap(value, bit):
    count = lax.axis_size("seq")
    return lax.ppermute(value, "seq", [(i, i ^ bit) for i in range(count)])


def from_plane_before(value):
    count = lax.axis_size("seq")
    return lax.ppermute(value, "seq", [(i, i + PLANE) for i in range(count - PLANE)])


def pack_kernel(*refs):
    *parts, gain, out = refs
    total = parts[0][...].astype(jnp.float32)
    for part in parts[1:]:
        total = total + part[...].astype(jnp.float32)
    head_dim = gain.shape[1]
    out[:, :head_dim] = rms_scale(total[:, :head_dim], gain[...]).astype(out.dtype)
    out[:, head_dim:] = total[:, head_dim:].astype(out.dtype)


def pack(parts, gain):
    tokens, columns = parts[0].shape
    head_dim = gain.shape[1]
    spec = pl.BlockSpec((tokens, 2 * head_dim), lambda h: (0, h))
    return pl.pallas_call(
        pack_kernel,
        grid=(columns // (2 * head_dim),),
        out_shape=jax.ShapeDtypeStruct((tokens, columns), jnp.bfloat16),
        in_specs=[spec] * len(parts) + [pl.BlockSpec((1, head_dim), lambda h: (0, 0))],
        out_specs=spec,
        compiler_params=pltpu.CompilerParams(vmem_limit_bytes=40 << 20),
        cost_estimate=pl.CostEstimate(
            flops=10 * tokens * columns, bytes_accessed=8 * tokens * columns, transcendentals=0
        ),
    )(*parts, gain)


def attend_kernel(n_parts, slots, tile, *refs):
    flags = refs[0]
    parts = refs[1 : 1 + n_parts]
    gain = refs[1 + n_parts]
    images = refs[2 + n_parts : 2 + n_parts + slots]
    out, q_ref, m_ref, l_ref, acc_ref = refs[2 + n_parts + slots :]
    rows = out.shape[0]
    head_dim = gain.shape[1]
    group = out.shape[1] // head_dim
    scale = math.log2(math.e) / math.sqrt(head_dim)
    for j in range(group):
        cols = slice(j * head_dim, (j + 1) * head_dim)
        total = parts[0][:, cols].astype(jnp.float32)
        for part in parts[1:]:
            total = total + part[:, cols].astype(jnp.float32)
        q_ref[j * rows : (j + 1) * rows, :] = rms_scale(total, gain[...]).astype(jnp.bfloat16)

    def one_image(slot):
        image = images[slot]

        @pl.loop(0, group * rows // tile)
        def _(t):
            at = pl.ds(pl.multiple_of(t * tile, tile), tile)
            scores = lax.dot_general(
                q_ref[at, :],
                image[:, :head_dim],
                (((1,), (1,)), ((), ())),
                preferred_element_type=jnp.float32,
            )
            peak = jnp.max(scores, axis=1, keepdims=True)
            if slot > 0:
                before = m_ref[at, :]
                peak = jnp.maximum(peak, before)
            weights = jnp.exp2((scores - peak) * scale)
            total = jnp.sum(weights, axis=1, keepdims=True)
            blended = jnp.dot(
                weights.astype(jnp.bfloat16),
                image[:, head_dim:],
                preferred_element_type=jnp.float32,
            )
            if slot > 0:
                kept = jnp.exp2((before - peak) * scale)
                total = total + kept * l_ref[at, :]
                blended = blended + kept * acc_ref[at, :]
            m_ref[at, :] = peak
            l_ref[at, :] = total
            acc_ref[at, :] = blended

    one_image(0)
    for slot in range(1, slots):
        pl.when(flags[slot] == 1)(lambda slot=slot: one_image(slot))
    for j in range(group):
        at = slice(j * rows, (j + 1) * rows)
        out[:, j * head_dim : (j + 1) * head_dim] = (acc_ref[at, :] / l_ref[at, :]).astype(out.dtype)


def attend(flags, parts, gain, images, first, heads):
    rows = parts[0].shape[0]
    tokens = images[0].shape[0]
    head_dim = gain.shape[1]
    group = parts[0].shape[1] // head_dim // first[1]
    width = group * head_dim
    start = first[0]
    slots = len(images)
    tall = group * rows
    tile = min(512, tall)

    def kernel(*refs):
        attend_kernel(len(parts), slots, tile, *refs)

    return pl.pallas_call(
        kernel,
        grid=(heads,),
        out_shape=jax.ShapeDtypeStruct((rows, heads * width), jnp.bfloat16),
        in_specs=[pl.BlockSpec(memory_space=pltpu.SMEM)]
        + [pl.BlockSpec((rows, width), lambda h: (0, h + start))] * len(parts)
        + [pl.BlockSpec((1, head_dim), lambda h: (0, 0))]
        + [pl.BlockSpec((tokens, 2 * head_dim), lambda h: (0, h))] * slots,
        out_specs=pl.BlockSpec((rows, width), lambda h: (0, h)),
        scratch_shapes=[
            pltpu.VMEM((tall, head_dim), jnp.bfloat16),
            pltpu.VMEM((tall, 1), jnp.float32),
            pltpu.VMEM((tall, 1), jnp.float32),
            pltpu.VMEM((tall, head_dim), jnp.float32),
        ],
        compiler_params=pltpu.CompilerParams(vmem_limit_bytes=48 << 20),
        cost_estimate=pl.CostEstimate(
            flops=12 * heads * tall * tokens * head_dim,
            bytes_accessed=4 * slots * heads * tokens * head_dim,
            transcendentals=3 * heads * tall * tokens,
        ),
    )(flags, *parts, gain, *images)


def on_device(
    text_states,
    images,
    norm_gain,
    query_weight,
    image_projection_weight,
    query_gain,
    key_gain,
    admission,
):
    head_dim = query_gain.shape[0]
    fsdp = lax.axis_size("fsdp")
    seq = lax.axis_size("seq")
    planes = seq // PLANE
    local_kv = KEY_VALUE_HEADS // fsdp
    rows, model = text_states.shape
    depth = query_weight.shape[0]
    index = lax.axis_index("seq")
    mine = lax.axis_index("fsdp")
    place = index % PLANE
    x_place = place // 2
    core = place % 2

    normed = rms_scale(text_states.astype(jnp.float32), norm_gain).astype(jnp.bfloat16)
    by_place = normed.reshape(rows, planes, PLANE, depth)

    def features_of(where):
        part = lax.dynamic_slice_in_dim(by_place, where, 1, 2)
        return part.reshape(rows, planes * depth)

    text_parts = [features_of(place)]
    for bit in range(1, PLANE):
        text_parts.append(swap(features_of(place ^ bit), bit))

    weight_block = lax.all_gather(image_projection_weight, "seq", axis=0, tiled=True)
    query_weight, weight_block = lax.optimization_barrier((query_weight, weight_block))
    groups = [[z * PLANE + p for z in range(planes)] for p in range(PLANE)]
    query_block = lax.all_gather(
        query_weight, "seq", axis=0, tiled=True, axis_index_groups=groups
    )

    features = images[0]
    chunks = 2 if local_kv % 2 == 0 else 1
    heads = local_kv // chunks
    width = heads * 2 * head_dim

    def project(owner, chunk):
        start = owner * (local_kv * 2 * head_dim) + chunk * width
        columns = lax.dynamic_slice_in_dim(weight_block, start, width, 1)
        return jnp.dot(features, columns, preferred_element_type=jnp.float32).astype(jnp.bfloat16)

    def rotate(value, steps):
        return lax.ppermute(value, "fsdp", [(i, (i + steps) % fsdp) for i in range(fsdp)])

    gain_row = key_gain.reshape(1, head_dim)
    sent = [
        [rotate(project((mine + s) % fsdp, c), s) for s in range(1, fsdp)] for c in range(chunks)
    ]
    windows = []
    for c in range(chunks):
        own = pack([project(mine, c)] + sent[c], gain_row)
        before = from_plane_before(own)
        two = swap(jnp.where(x_place == 0, own, before), 2)
        near = swap(jnp.where(core == 0, own, before), 1)
        far = swap(two, 1)
        windows.append([own, before, two, near, far])

    partial = jnp.dot(
        jnp.concatenate(text_parts, axis=0), query_block, preferred_element_type=jnp.float32
    ).astype(jnp.bfloat16)
    query_parts = [partial[:rows]]
    for bit in range(1, PLANE):
        query_parts.append(swap(partial[bit * rows : (bit + 1) * rows], bit))

    near_by = jnp.where(core == 0, 3, 1)
    far_by = jnp.where(core == 0, 1, 3)
    distances = jnp.stack(
        [jnp.int32(0), jnp.int32(PLANE), jnp.int32(2), near_by.astype(jnp.int32), far_by.astype(jnp.int32)]
    )
    image_ids = index - distances
    flags = (image_ids >= 0) & (jnp.take(admission[0], jnp.maximum(image_ids, 0)) == 1)
    flags = flags.astype(jnp.int32)
    outs = [
        attend(
            flags, query_parts, query_gain.reshape(1, head_dim), windows[c], (c * heads, local_kv), heads
        )
        for c in range(chunks)
    ]
    return jnp.concatenate(outs, axis=1) if chunks > 1 else outs[0]


def solution(mesh):
    placed = (
        P("seq", None),
        P("seq", None, "fsdp"),
        P(),
        P("seq", "fsdp"),
        P(("fsdp", "seq"), None),
        P(),
        P(),
        P("seq", None),
    )
    return jax.shard_map(
        on_device, mesh=mesh, in_specs=placed, out_specs=P("seq", "fsdp"), check_vma=False
    )
```

time: 953 us -> 582 us (0.61)
  waiting for transfers between devices: 587 us -> 403 us
  matrix products: 173 us -> 56.7 us
  local copies, waits for them, and re-layouts: 93.5 us -> 11.5 us
  Pallas kernels: 0 us -> 65.1 us
  other arithmetic: 77.4 us -> 13.3 us
    dot_general x10 -> x5, matrix products: 173 us -> 56.7 us  [the longest x4 44.3 us: project(): jnp.dot(features, columns, preferred_element_type=jnp.float32)]
    ppermute x4 -> x16, waiting for transfers between devices: 378 us -> 275 us  [the longest x12 120 us: swap(): return lax.ppermute(value, 'seq', [(i, i ^ bit) for i in range(count)])]
    reduce_scatter x1 -> x0, waiting for transfers between devices: 80.4 us -> none  [on_device(): lax.psum_scatter(score_product.reshape(features.shape[0], local_key_value...]
    pallas_call x0 -> x4, Pallas kernels: none -> 65.1 us  [the longest x2 62.8 us: attend(): pl.pallas_call(kernel, grid=(heads,), out_shape=jax.ShapeDtypeStruct((row...]
    reduce_sum x7 -> x1, other arithmetic: 67.7 us -> 3.34 us  [rms_scale(): jnp.mean(values * values, axis=-1, keepdims=True) + EPS]
    dot_general x1 -> x0, local copies, waits for them, and re-layouts: 20.8 us -> none  [on_device(): jnp.dot(features, columns, preferred_element_type=jnp.float32)]
    squeeze x4 -> x0, local copies, waits for them, and re-layouts: 17.4 us -> none  [attend(): outputs = lax.map(one_head, (grouped, per_head))]
    reshape x2 -> x0, local copies, waits for them, and re-layouts: 15.4 us -> none  [the longest x1 12.7 us: attend(): jnp.moveaxis(stacked, 1, 0)]
  transfers between devices with their start and end apart: 7 -> 18, of which waited for: 5 -> 8; matrix products, arithmetic and copies ran while one was open for 5% -> 14% of each run, Pallas kernels for 0% -> 6%
where the time goes in v1:
time: 582 us; the launch traced here: 575 us
  waiting for transfers between devices  403 us (69%)
  Pallas kernels  65.1 us (11%)
  matrix products  56.7 us (10%)
  between operations  14.1 us (2%)
  other arithmetic  13.3 us (2%)
  local copies, waits for them, and re-layouts  11.5 us (2%)
  starting transfers between devices  11.1 us (2%)
    all_gather x1, waiting for transfers between devices, on_device(): lax.all_gather(image_projection_weight, 'seq', axis=0, tiled=True)  128 us
    ppermute x12, waiting for transfers between devices, swap(): return lax.ppermute(value, 'seq', [(i, i ^ bit) for i in range(count)])  120 us
    ppermute x2, waiting for transfers between devices, from_plane_before(): lax.ppermute(value, 'seq', [(i, i + PLANE) for i in range(count - PLANE)])  105 us
    pallas_call x2, Pallas kernels, attend(): pl.pallas_call(kernel, grid=(heads,), out_shape=jax.ShapeDtypeStruct((row...  62.8 us
    ppermute x2, waiting for transfers between devices, rotate(): lax.ppermute(value, 'fsdp', [(i, (i + steps) % fsdp) for i in range(fsdp)])  49.7 us
    dot_general x4, matrix products, project(): jnp.dot(features, columns, preferred_element_type=jnp.float32)  44.3 us
    dot_general x1, matrix products, on_device(): jnp.dot(jnp.concatenate(text_parts, axis=0), query_block, preferred_eleme...  12.3 us
  transfers between devices with their start and end apart: 18, of which 8 were waited for; matrix products, arithmetic and copies ran while one was open for 14% of the time, Pallas kernels for 6%

profile of v1, /device:TPU:27, one launch (start us, length us, event | category | flops | bytes accessed | tf_op | source)
XLA Modules:
  0.0 574.9 jit_solution(1328918761928860731)
XLA Ops:
  7.3 127.6 %all-gather.3.cloned.1.call-done = bf16[4096,2048]{1,0:T(8,128)(2,1)} async-done(((bf16[256,2048]{1,0:T(8,128)(2,1)}), bf16[4096,2048]{1,0:T(8,128)(2,1)}) %all-gather.3.cloned.1.call-update) | async-done | bytes 16777232 | tf_op jit(solution)/shard_map/all_gather | solution.py:185
  135.0 11.5 %fusion.56 = bf16[1601,512]{1,0:T(8,128)(2,1)S(1)} fusion(bf16[1,1601,4096]{2,1,0:T(8,128)(2,1)} %param.9, bf16[4096,2048]{1,0:T(8,128)(2,1)} %all-gather.3.cloned.1.call-done, s32[]{:T(128)S(6)} %select_n.92), kind=kOutput, calls=%fused_computation.33 | convolution fusion | flops 6715900416 | bytes 19006468 | tf_op jit(solution)/shard_map/dot_general | solution.py:200
  147.8 10.2 %fusion.46 = bf16[1601,512]{1,0:T(8,128)(2,1)} fusion(bf16[1,1601,4096]{2,1,0:T(8,128)(2,1)S(1)} %bitcast.59, bf16[4096,2048]{1,0:T(8,128)(2,1)} %all-gather.3.cloned.1.call-done, s32[]{:T(128)S(6)} %select_n.99), kind=kOutput, calls=%fused_computation.31 | convolution fusion | flops 6715900416 | bytes 18949124 | tf_op jit(solution)/shard_map/dot_general | solution.py:200
  158.3 11.3 %fusion.51.refs_0_ = bf16[1601,512]{1,0:T(8,128)(2,1)S(1)} fusion(bf16[1,1601,4096]{2,1,0:T(8,128)(2,1)} %param.9, bf16[4096,2048]{1,0:T(8,128)(2,1)} %all-gather.3.cloned.1.call-done, s32[]{:T(128)S(6)} %select_n.98), kind=kOutput, calls=%fused_computation.32 | convolution fusion | flops 6715900416 | bytes 19006468 | tf_op jit(solution)/shard_map/dot_general | solution.py:200
  169.6 49.7 %collective-permute-done.11.refs_1_ = bf16[1601,512]{1,0:T(8,128)(2,1)S(1)} collective-permute-done((bf16[1601,512]{1,0:T(8,128)(2,1)}, bf16[1601,512]{1,0:T(8,128)(2,1)S(1)}, u32[]{:S(2)}, u32[]{:S(2)}) %collective-permute-start.11) | collective-permute-done | bytes 1639456 | tf_op jit(solution)/shard_map/ppermute | solution.py:203
  220.4 1.5 collective-permute-start.12
  221.9 11.4 %fusion.61.refs_0_ = bf16[1601,512]{1,0:T(8,128)(2,1)S(1)} fusion(bf16[1,1601,4096]{2,1,0:T(8,128)(2,1)} %param.9, bf16[4096,2048]{1,0:T(8,128)(2,1)} %all-gather.3.cloned.1.call-done, s32[]{:T(128)S(6)} %select_n.90), kind=kOutput, calls=%fused_computation.34 | convolution fusion | flops 6715900416 | bytes 19006468 | tf_op jit(solution)/shard_map/dot_general | solution.py:200
  235.8 6.4 %copy.9 = bf16[256,8192]{0,1:T(8,128)(2,1)} copy(bf16[256,8192]{1,0:T(8,128)(2,1)} %param.8) | data formatting | bytes 8388608 | tf_op args[0]
  242.3 3.3 fusion.8
  245.6 73.2 %collective-permute-done.12.refs_7_ = bf16[1601,512]{1,0:T(8,128)(2,1)} collective-permute-done((bf16[1601,512]{1,0:T(8,128)(2,1)S(1)}, bf16[1601,512]{1,0:T(8,128)(2,1)}, u32[]{:S(2)}, u32[]{:S(2)}) %collective-permute-start.12) | collective-permute-done | bytes 1639456 | tf_op jit(solution)/shard_map/ppermute | solution.py:27
  318.9 3.4 broadcast_select_fusion
  322.5 31.6 %collective-permute-done.7.refs_7_ = bf16[1601,512]{1,0:T(8,128)(2,1)} collective-permute-done((bf16[1601,512]{1,0:T(8,128)(2,1)S(1)}, bf16[1601,512]{1,0:T(8,128)(2,1)}, u32[]{:S(2)}, u32[]{:S(2)}) %collective-permute-start.7) | collective-permute-done | bytes 1639456 | tf_op jit(solution)/shard_map/ppermute | solution.py:27
  354.1 2.8 broadcast_select_fusion.1
  357.2 2.6 fusion.10
  359.8 2.4 constant_dynamic-slice_fusion.3
  362.3 1.8 collective-permute-start.2
  364.6 54.1 %collective-permute-done.2 = bf16[256,2048]{0,1:T(8,128)(2,1)S(1)} collective-permute-done((bf16[256,2048]{0,1:T(8,128)(2,1)S(1)}, bf16[256,2048]{0,1:T(8,128)(2,1)S(1)}, u32[]{:S(2)}, u32[]{:S(2)}) %collective-permute-start.2) | collective-permute-done | bytes 1048608 | tf_op jit(solution)/shard_map/ppermute | solution.py:22
  418.7 21.3 %collective-permute-done.1 = bf16[256,2048]{0,1:T(8,128)(2,1)S(1)} collective-permute-done((bf16[256,2048]{0,1:T(8,128)(2,1)S(1)}, bf16[256,2048]{0,1:T(8,128)(2,1)S(1)}, u32[]{:S(2)}, u32[]{:S(2)}) %collective-permute-start.1) | collective-permute-done | bytes 1048608 | tf_op jit(solution)/shard_map/ppermute | solution.py:22
  441.6 12.3 %fusion.23 = bf16[1024,2048]{1,0:T(8,128)(2,1)S(1)} fusion(bf16[2048,2048]{1,0:T(8,128)(2,1)} %all-gather.5.cloned.1.call-done, bf16[256,2048]{0,1:T(8,128)(2,1)} %copy-done.7, bf16[256,2048]{0,1:T(8,128)(2,1)} %copy-done.8, bf16[256,2048]{0,1:T(8,128)(2,1)} %collective-permute-done, bf16[256,2048]{0,1:T(8,128)(2,1)S(1)} %bitcast.54), kind=kOutput, calls=%fused_computation.26 | convolution fusion | flops 8608808960 | bytes 16777216 | tf_op jit(solution)/shard_map/dot_general | solution.py:218
  454.0 1.8 fusion.71
  458.8 22.7 %collective-permute-done.5.refs_4_ = bf16[256,2048]{1,0:T(8,128)(2,1)S(1)} collective-permute-done((bf16[256,2048]{1,0:T(8,128)(2,1)}, bf16[256,2048]{1,0:T(8,128)(2,1)S(1)}, u32[]{:S(2)}, u32[]{:S(2)}) %collective-permute-start.5) | collective-permute-done | bytes 1048608 | tf_op jit(solution)/shard_map/ppermute | solution.py:22
  481.5 22.3 %collective-permute-done.4.refs_3_ = bf16[256,2048]{1,0:T(8,128)(2,1)S(1)} collective-permute-done((bf16[256,2048]{1,0:T(8,128)(2,1)}, bf16[256,2048]{1,0:T(8,128)(2,1)S(1)}, u32[]{:S(2)}, u32[]{:S(2)}) %collective-permute-start.4) | collective-permute-done | bytes 1048608 | tf_op jit(solution)/shard_map/ppermute | solution.py:22
  503.8 31.4 %shard_map.85 = bf16[256,1024]{1,0:T(8,128)(2,1)S(1)} custom-call(s32[5]{0:T(128)S(1)} %and_convert_fusion.refs_0_, bf16[256,2048]{1,0:T(8,128)(2,1)S(1)} %get-tuple-element.12.refs_1_, bf16[256,2048]{1,0:T(8,128)(2,1)} %collective-permute-done.3.refs_2_, bf16[256,2048]{1,0:T(8,128)(2,1)S(1)} %collective-permute-done.4.refs_3_, ...), custom_call_target="tpu_custom_call" | custom-call | flops 5036310528 | bytes 8197120 | tf_op jit(solution)/shard_map/pallas_call | solution.py:127
  535.2 31.4 %shard_map.83 = bf16[256,1024]{1,0:T(8,128)(2,1)S(1)} custom-call(s32[5]{0:T(128)S(1)} %and_convert_fusion.refs_0_, bf16[256,2048]{1,0:T(8,128)(2,1)S(1)} %get-tuple-element.12.refs_1_, bf16[256,2048]{1,0:T(8,128)(2,1)} %collective-permute-done.3.refs_2_, bf16[256,2048]{1,0:T(8,128)(2,1)S(1)} %collective-permute-done.4.refs_3_, ...), custom_call_target="tpu_custom_call" | custom-call | flops 5036310528 | bytes 8197120 | tf_op jit(solution)/shard_map/pallas_call | solution.py:127
  (65 shorter events, 12.8 us)
Async XLA Ops:
  6.5 451.5 %copy-start = (s32[1,16]{1,0:T(1,128)S(1)}, s32[1,16]{1,0:T(1,128)}, u32[]{:S(2)}) copy-start(s32[1,16]{1,0:T(1,128)} %param.15) | copy-start | bytes 196
  6.5 128.4 %all-gather.3.cloned.1.call-start = ((), (), s32[]{:S(2)}) async-start(), calls=%async_computation | async-start | bytes 17825792 | tf_op jit(solution)/shard_map/all_gather | solution.py:185
  7.3 434.4 %all-gather.5.cloned.1.call-start = ((), (), s32[]{:S(2)}) async-start(), calls=%async_computation.1 | async-start | bytes 10485760 | tf_op jit(solution)/shard_map/all_gather | solution.py:188
  146.4 86.8 %collective-permute-start.6 = (bf16[1601,512]{1,0:T(8,128)(2,1)S(1)}, bf16[1601,512]{1,0:T(8,128)(2,1)S(1)}, u32[]{:S(2)}, u32[]{:S(2)}) collective-permute-start(bf16[1601,512]{1,0:T(8,128)(2,1)S(1)} %fusion.56), channel_id=1, source_target_pairs={{0,1},{1,0},{2,3},{3,2},{4,5},{5,4},{6,7},{7,6},{8,9},{9,8},{10,11... | collective-permute-start | bytes 4918280 | tf_op jit(solution)/shard_map/ppermute | solution.py:203
  158.0 61.3 %copy-start.3 = (f32[128]{0:T(128)S(1)}, f32[128]{0:T(128)}, u32[]{:S(2)}) copy-start(f32[128]{0:T(128)} %param.14) | copy-start | bytes 1540
  158.0 61.3 %collective-permute-start.11 = (bf16[1601,512]{1,0:T(8,128)(2,1)}, bf16[1601,512]{1,0:T(8,128)(2,1)S(1)}, u32[]{:S(2)}, u32[]{:S(2)}) collective-permute-start(bf16[1601,512]{1,0:T(8,128)(2,1)} %fusion.46), channel_id=1, source_target_pairs={{0,1},{1,0},{2,3},{3,2},{4,5},{5,4},{6,7},{7,6},{8,9},{9,8},{10,11... | collective-permute-start | bytes 4918280 | tf_op jit(solution)/shard_map/ppermute | solution.py:203
  220.4 98.4 %copy-start.1 = (bf16[1601,512]{1,0:T(8,128)(2,1)}, bf16[1601,512]{1,0:T(8,128)(2,1)S(1)}, u32[]{:S(2)}) copy-start(bf16[1601,512]{1,0:T(8,128)(2,1)S(1)} %shard_map.84.refs_6_) | copy-start | bytes 4918276
  220.4 98.4 %collective-permute-start.12 = (bf16[1601,512]{1,0:T(8,128)(2,1)S(1)}, bf16[1601,512]{1,0:T(8,128)(2,1)}, u32[]{:S(2)}, u32[]{:S(2)}) collective-permute-start(bf16[1601,512]{1,0:T(8,128)(2,1)S(1)} %shard_map.84.refs_6_), channel_id=1, source_target_pairs={{0,8},{2,10},{4,12},{6,14},{8,16},{10,18},{12,20},{14,22},{16,24},... | collective-permute-start | bytes 4918280 | tf_op jit(solution)/shard_map/ppermute | solution.py:27
  234.5 119.7 %copy-start.2 = (bf16[1601,512]{1,0:T(8,128)(2,1)}, bf16[1601,512]{1,0:T(8,128)(2,1)S(1)}, u32[]{:S(2)}) copy-start(bf16[1601,512]{1,0:T(8,128)(2,1)S(1)} %shard_map.82.refs_6_) | copy-start | bytes 4918276
  234.5 119.6 %collective-permute-start.7 = (bf16[1601,512]{1,0:T(8,128)(2,1)S(1)}, bf16[1601,512]{1,0:T(8,128)(2,1)}, u32[]{:S(2)}, u32[]{:S(2)}) collective-permute-start(bf16[1601,512]{1,0:T(8,128)(2,1)S(1)} %shard_map.82.refs_6_), channel_id=1, source_target_pairs={{0,8},{2,10},{4,12},{6,14},{8,16},{10,18},{12,20},{14,22},{16,24},... | collective-permute-start | bytes 4918280 | tf_op jit(solution)/shard_map/ppermute | solution.py:27
  322.3 35.0 %copy-start.6 = (f32[8192]{0:T(1024)S(1)}, f32[8192]{0:T(1024)}, u32[]{:S(2)}) copy-start(f32[8192]{0:T(1024)} %param.10) | copy-start | bytes 98308
  322.3 118.8 %collective-permute-start.13 = (bf16[1601,512]{1,0:T(8,128)(2,1)}, bf16[1601,512]{1,0:T(8,128)(2,1)}, u32[]{:S(2)}, u32[]{:S(2)}) collective-permute-start(bf16[1601,512]{1,0:T(8,128)(2,1)} %get-tuple-element.20), channel_id=1, source_target_pairs={{0,4},{2,6},{4,0},{6,2},{8,12},{10,14},{12,8},{14,10},{16,20},{18,... | collective-permute-start | bytes 4918280 | tf_op jit(solution)/shard_map/ppermute | solution.py:22
  357.0 84.2 %collective-permute-start.8 = (bf16[1601,512]{1,0:T(8,128)(2,1)S(1)}, bf16[1601,512]{1,0:T(8,128)(2,1)}, u32[]{:S(2)}, u32[]{:S(2)}) collective-permute-start(bf16[1601,512]{1,0:T(8,128)(2,1)S(1)} %get-tuple-element.18), channel_id=1, source_target_pairs={{0,4},{2,6},{4,0},{6,2},{8,12},{10,14},{12,8},{14,10},{16,20},{18,... | collective-permute-start | bytes 4918280 | tf_op jit(solution)/shard_map/ppermute | solution.py:22
  362.3 56.4 %collective-permute-start.2 = (bf16[256,2048]{0,1:T(8,128)(2,1)S(1)}, bf16[256,2048]{0,1:T(8,128)(2,1)S(1)}, u32[]{:S(2)}, u32[]{:S(2)}) collective-permute-start(bf16[256,2048]{0,1:T(8,128)(2,1)S(1)} %bitcast.57), channel_id=1, source_target_pairs={{0,6},{2,4},{4,2},{6,0},{8,14},{10,12},{12,10},{14,8},{16,22},{18,... | collective-permute-start | bytes 3145736 | tf_op jit(solution)/shard_map/ppermute | solution.py:22
  364.1 75.8 %collective-permute-start.1 = (bf16[256,2048]{0,1:T(8,128)(2,1)S(1)}, bf16[256,2048]{0,1:T(8,128)(2,1)S(1)}, u32[]{:S(2)}, u32[]{:S(2)}) collective-permute-start(bf16[256,2048]{0,1:T(8,128)(2,1)S(1)} %bitcast.56), channel_id=1, source_target_pairs={{0,4},{2,6},{4,0},{6,2},{8,12},{10,14},{12,8},{14,10},{16,20},{18,... | collective-permute-start | bytes 3145736 | tf_op jit(solution)/shard_map/ppermute | solution.py:22
  364.4 77.2 %collective-permute-start = (bf16[256,2048]{0,1:T(8,128)(2,1)S(1)}, bf16[256,2048]{0,1:T(8,128)(2,1)}, u32[]{:S(2)}, u32[]{:S(2)}) collective-permute-start(bf16[256,2048]{0,1:T(8,128)(2,1)S(1)} %bitcast.55), channel_id=1, source_target_pairs={{0,2},{2,0},{4,6},{6,4},{8,10},{10,8},{12,14},{14,12},{16,18},{18,... | collective-permute-start | bytes 3145736 | tf_op jit(solution)/shard_map/ppermute | solution.py:22
  418.7 37.7 %collective-permute-start.14 = (bf16[1601,512]{1,0:T(8,128)(2,1)}, bf16[1601,512]{1,0:T(8,128)(2,1)}, u32[]{:S(2)}, u32[]{:S(2)}) collective-permute-start(bf16[1601,512]{1,0:T(8,128)(2,1)} %get-tuple-element.19), channel_id=1, source_target_pairs={{0,2},{2,0},{4,6},{6,4},{8,10},{10,8},{12,14},{14,12},{16,18},{18,... | collective-permute-start | bytes 4918280 | tf_op jit(solution)/shard_map/ppermute | solution.py:22
  440.0 95.2 %collective-permute-start.9 = (bf16[1601,512]{1,0:T(8,128)(2,1)}, bf16[1601,512]{1,0:T(8,128)(2,1)}, u32[]{:S(2)}, u32[]{:S(2)}) collective-permute-start(bf16[1601,512]{1,0:T(8,128)(2,1)} %get-tuple-element.17), channel_id=1, source_target_pairs={{0,2},{2,0},{4,6},{6,4},{8,10},{10,8},{12,14},{14,12},{16,18},{18,... | collective-permute-start | bytes 4918280 | tf_op jit(solution)/shard_map/ppermute | solution.py:22
  441.1 16.5 %collective-permute-start.15 = (bf16[1601,512]{1,0:T(8,128)(2,1)}, bf16[1601,512]{1,0:T(8,128)(2,1)}, u32[]{:S(2)}, u32[]{:S(2)}) collective-permute-start(bf16[1601,512]{1,0:T(8,128)(2,1)} %collective-permute-done.13.refs_8_), channel_id=1, source_target_pairs={{0,2},{2,0},{4,6},{6,4},{8,10},{10,8},{12,14},{14,12},{16,18},{18,... | collective-permute-start | bytes 4918280 | tf_op jit(solution)/shard_map/ppermute | solution.py:22
  441.2 94.0 %collective-permute-start.10 = (bf16[1601,512]{1,0:T(8,128)(2,1)}, bf16[1601,512]{1,0:T(8,128)(2,1)}, u32[]{:S(2)}, u32[]{:S(2)}) collective-permute-start(bf16[1601,512]{1,0:T(8,128)(2,1)} %collective-permute-done.8.refs_8_), channel_id=1, source_target_pairs={{0,2},{2,0},{4,6},{6,4},{8,10},{10,8},{12,14},{14,12},{16,18},{18,... | collective-permute-start | bytes 4918280 | tf_op jit(solution)/shard_map/ppermute | solution.py:22
  454.0 49.8 %copy-start.4 = (f32[128]{0:T(128)S(1)}, f32[128]{0:T(128)}, u32[]{:S(2)}) copy-start(f32[128]{0:T(128)} %param.13) | copy-start | bytes 1540
  455.8 25.7 %collective-permute-start.5 = (bf16[256,2048]{1,0:T(8,128)(2,1)}, bf16[256,2048]{1,0:T(8,128)(2,1)S(1)}, u32[]{:S(2)}, u32[]{:S(2)}) collective-permute-start(bf16[256,2048]{1,0:T(8,128)(2,1)} %get-tuple-element.9), channel_id=1, source_target_pairs={{0,6},{2,4},{4,2},{6,0},{8,14},{10,12},{12,10},{14,8},{16,22},{18,... | collective-permute-start | bytes 3145736 | tf_op jit(solution)/shard_map/ppermute | solution.py:22
  456.4 47.3 %collective-permute-start.4 = (bf16[256,2048]{1,0:T(8,128)(2,1)}, bf16[256,2048]{1,0:T(8,128)(2,1)S(1)}, u32[]{:S(2)}, u32[]{:S(2)}) collective-permute-start(bf16[256,2048]{1,0:T(8,128)(2,1)} %get-tuple-element.10), channel_id=1, source_target_pairs={{0,4},{2,6},{4,0},{6,2},{8,12},{10,14},{12,8},{14,10},{16,20},{18,... | collective-permute-start | bytes 3145736 | tf_op jit(solution)/shard_map/ppermute | solution.py:22
  457.6 46.2 %collective-permute-start.3 = (bf16[256,2048]{1,0:T(8,128)(2,1)}, bf16[256,2048]{1,0:T(8,128)(2,1)}, u32[]{:S(2)}, u32[]{:S(2)}) collective-permute-start(bf16[256,2048]{1,0:T(8,128)(2,1)} %get-tuple-element.11), channel_id=1, source_target_pairs={{0,2},{2,0},{4,6},{6,4},{8,10},{10,8},{12,14},{14,12},{16,18},{18,... | collective-permute-start | bytes 3145736 | tf_op jit(solution)/shard_map/ppermute | solution.py:22
  (7 other events, 110.4 us)
Sparse Core Ops, SparseCore 0:
  9.5 125.3 all-gather.2
  136.5 174.5 all-gather.4

commit v2 on v1

--- a/solution.py
+++ b/solution.py
@@ -110,13 +110,12 @@
         out[:, j * head_dim : (j + 1) * head_dim] = (acc_ref[at, :] / l_ref[at, :]).astype(out.dtype)
 
 
-def attend(flags, parts, gain, images, first, heads):
+def attend(flags, parts, gain, images, heads):
     rows = parts[0].shape[0]
     tokens = images[0].shape[0]
     head_dim = gain.shape[1]
-    group = parts[0].shape[1] // head_dim // first[1]
+    group = parts[0].shape[1] // head_dim // heads
     width = group * head_dim
-    start = first[0]
     slots = len(images)
     tall = group * rows
     tile = min(512, tall)
@@ -129,7 +128,7 @@
         grid=(heads,),
         out_shape=jax.ShapeDtypeStruct((rows, heads * width), jnp.bfloat16),
         in_specs=[pl.BlockSpec(memory_space=pltpu.SMEM)]
-        + [pl.BlockSpec((rows, width), lambda h: (0, h + start))] * len(parts)
+        + [pl.BlockSpec((rows, width), lambda h: (0, h))] * len(parts)
         + [pl.BlockSpec((1, head_dim), lambda h: (0, 0))]
         + [pl.BlockSpec((tokens, 2 * head_dim), lambda h: (0, h))] * slots,
         out_specs=pl.BlockSpec((rows, width), lambda h: (0, h)),
@@ -178,49 +177,93 @@
         part = lax.dynamic_slice_in_dim(by_place, where, 1, 2)
         return part.reshape(rows, planes * depth)
 
-    text_parts = [features_of(place)]
-    for bit in range(1, PLANE):
-        text_parts.append(swap(features_of(place ^ bit), bit))
-
-    weight_block = lax.all_gather(image_projection_weight, "seq", axis=0, tiled=True)
-    query_weight, weight_block = lax.optimization_barrier((query_weight, weight_block))
-    groups = [[z * PLANE + p for z in range(planes)] for p in range(PLANE)]
-    query_block = lax.all_gather(
-        query_weight, "seq", axis=0, tiled=True, axis_index_groups=groups
-    )
+    text_sources = [features_of(place ^ bit) for bit in range(PLANE)]
 
     features = images[0]
     chunks = 2 if local_kv % 2 == 0 else 1
     heads = local_kv // chunks
     width = heads * 2 * head_dim
-
-    def project(owner, chunk):
-        start = owner * (local_kv * 2 * head_dim) + chunk * width
-        columns = lax.dynamic_slice_in_dim(weight_block, start, width, 1)
-        return jnp.dot(features, columns, preferred_element_type=jnp.float32).astype(jnp.bfloat16)
+    query_width = query_weight.shape[1] // chunks
+    groups = [[z * PLANE + p for z in range(planes)] for p in range(PLANE)]
+
+    def columns_of(step, chunk):
+        start = (mine + step) % fsdp * (local_kv * 2 * head_dim) + chunk * width
+        return lax.dynamic_slice_in_dim(image_projection_weight, start, width, 1)
+
+    order = [(s, c) for s in range(1, fsdp) for c in range(chunks)] + [(0, c) for c in range(chunks)]
+    query_shards = [
+        query_weight[:, c * query_width : (c + 1) * query_width] for c in range(chunks)
+    ]
+    gathered = []
+
+    def gather(shard, after=(), **options):
+        if gathered:
+            shard, gathered[-1], after = lax.optimization_barrier((shard, gathered[-1], after))
+        gathered.append(lax.all_gather(shard, "seq", axis=0, tiled=True, **options))
+        return after
+
+    def project(step):
+        product = jnp.dot(features, gathered[step], preferred_element_type=jnp.float32)
+        return product.astype(jnp.bfloat16)
 
     def rotate(value, steps):
         return lax.ppermute(value, "fsdp", [(i, (i + steps) % fsdp) for i in range(fsdp)])
 
     gain_row = key_gain.reshape(1, head_dim)
-    sent = [
-        [rotate(project((mine + s) % fsdp, c), s) for s in range(1, fsdp)] for c in range(chunks)
-    ]
+    sent = {}
     windows = []
-    for c in range(chunks):
-        own = pack([project(mine, c)] + sent[c], gain_row)
-        before = from_plane_before(own)
+    text = None
+    gather(columns_of(*order[0]))
+    for step, key in enumerate(order):
+        later = order[step + 1] if step + 1 < len(order) else None
+        if step == 0:
+            text_sources = gather(columns_of(*later), text_sources)
+            text_parts = text_sources[:1]
+            for bit in range(1, PLANE):
+                text_parts.append(swap(text_sources[bit], bit))
+        else:
+            if step == 1:
+                after = text_parts
+            else:
+                after = [sent[order[step - 2]]] if order[step - 2] in sent else []
+            if later is not None:
+                after = gather(columns_of(*later), after)
+            else:
+                after = gather(query_shards[0], after, axis_index_groups=groups)
+            if step == 1:
+                text = jnp.concatenate(after, axis=0)
+            elif after:
+                sent[order[step - 2]] = after[0]
+        if key[0] > 0:
+            sent[key] = rotate(project(step), key[0])
+        else:
+            own = pack([project(step)] + [sent[s, key[1]] for s in range(1, fsdp)], gain_row)
+            before = from_plane_before(own)
+            windows.append([own, before])
+
+    def relay(own, before):
         two = swap(jnp.where(x_place == 0, own, before), 2)
         near = swap(jnp.where(core == 0, own, before), 1)
-        far = swap(two, 1)
-        windows.append([own, before, two, near, far])
-
-    partial = jnp.dot(
-        jnp.concatenate(text_parts, axis=0), query_block, preferred_element_type=jnp.float32
-    ).astype(jnp.bfloat16)
-    query_parts = [partial[:rows]]
-    for bit in range(1, PLANE):
-        query_parts.append(swap(partial[bit * rows : (bit + 1) * rows], bit))
+        return [own, before, two, near]
+
+    windows[0] = relay(*windows[0])
+    for shard in query_shards[1:]:
+        windows[0][2], windows[1][1] = gather(
+            shard, [windows[0][2], windows[1][1]], axis_index_groups=groups
+        )
+    windows[1:] = [relay(*window) for window in windows[1:]]
+    for window in windows:
+        window.append(swap(window[2], 1))
+    query_blocks = gathered[len(order) :]
+
+    query_parts = []
+    for c in range(chunks):
+        partial = jnp.dot(text, query_blocks[c], preferred_element_type=jnp.float32)
+        partial = partial.astype(jnp.bfloat16)
+        parts = [partial[:rows]]
+        for bit in range(1, PLANE):
+            parts.append(swap(partial[bit * rows : (bit + 1) * rows], bit))
+        query_parts.append(parts)
 
     near_by = jnp.where(core == 0, 3, 1)
     far_by = jnp.where(core == 0, 1, 3)
@@ -232,7 +275,7 @@
     flags = flags.astype(jnp.int32)
     outs = [
         attend(
-            flags, query_parts, query_gain.reshape(1, head_dim), windows[c], (c * heads, local_kv), heads
+            flags, query_parts[c], query_gain.reshape(1, head_dim), windows[c], heads
         )
         for c in range(chunks)
     ]

time: 582 us -> 563 us (0.967)
  waiting for transfers between devices: 403 us -> 367 us
  local copies, waits for them, and re-layouts: 11.5 us -> 22 us
  starting transfers between devices: 11.1 us -> 17.4 us
    all_gather x2 -> x6, waiting for transfers between devices: 128 us -> 61.3 us  [gather(): gathered.append(lax.all_gather(shard, 'seq', axis=0, tiled=True, **options))]
    ppermute x2, waiting for transfers between devices: 49.7 us -> 70.9 us  [rotate(): lax.ppermute(value, 'fsdp', [(i, (i + steps) % fsdp) for i in range(fsdp)])]
    ppermute x2, waiting for transfers between devices: 105 us -> 113 us  [from_plane_before(): lax.ppermute(value, 'seq', [(i, i + PLANE) for i in range(count - PLANE)])]
    unnamed x27 -> x40, local copies, waits for them, and re-layouts: 6.48 us -> 12.9 us
    ppermute x12 -> x15, starting transfers between devices: 6.66 us -> 11.7 us  [swap(): return lax.ppermute(value, 'seq', [(i, i ^ bit) for i in range(count)])]
    ppermute x12 -> x15, waiting for transfers between devices: 120 us -> 123 us  [swap(): return lax.ppermute(value, 'seq', [(i, i ^ bit) for i in range(count)])]
    dot_general x5 -> x6, matrix products: 56.7 us -> 57 us  [the longest x4 44.2 us: project(): jnp.dot(features, gathered[step], preferred_element_type=jnp.float32)]
  transfers between devices with their start and end apart: 18 -> 25, of which waited for: 8 -> 14; matrix products, arithmetic and copies ran while one was open for 14% -> 15% of each run, Pallas kernels for 6% -> 6%
where the time goes in v2:
time: 563 us; the launch traced here: 556 us
  waiting for transfers between devices  367 us (65%)
  Pallas kernels  64.7 us (11%)
  matrix products  57 us (10%)
  local copies, waits for them, and re-layouts  22 us (4%)
  starting transfers between devices  17.4 us (3%)
  between operations  14.4 us (3%)
  other arithmetic  12.9 us (2%)
    ppermute x15, waiting for transfers between devices, swap(): return lax.ppermute(value, 'seq', [(i, i ^ bit) for i in range(count)])  123 us
    ppermute x2, waiting for transfers between devices, from_plane_before(): lax.ppermute(value, 'seq', [(i, i + PLANE) for i in range(count - PLANE)])  113 us
    ppermute x2, waiting for transfers between devices, rotate(): lax.ppermute(value, 'fsdp', [(i, (i + steps) % fsdp) for i in range(fsdp)])  70.9 us
    pallas_call x2, Pallas kernels, attend(): pl.pallas_call(kernel, grid=(heads,), out_shape=jax.ShapeDtypeStruct((row...  62.3 us
    all_gather x6, waiting for transfers between devices, gather(): gathered.append(lax.all_gather(shard, 'seq', axis=0, tiled=True, **options))  61.3 us
    dot_general x4, matrix products, project(): jnp.dot(features, gathered[step], preferred_element_type=jnp.float32)  44.2 us
    unnamed x40, local copies, waits for them, and re-layouts  12.9 us
    dot_general x2, matrix products, on_device(): partial = jnp.dot(text, query_blocks[c], preferred_element_type=jnp.float32)  12.8 us
  transfers between devices with their start and end apart: 25, of which 14 were waited for; matrix products, arithmetic and copies ran while one was open for 15% of the time, Pallas kernels for 6%

profile of v2, /device:TPU:27, one launch (start us, length us, event | category | flops | bytes accessed | tf_op | source)
XLA Modules:
  0.0 555.8 jit_solution(12683389188132266622)
XLA Ops:
  8.9 6.4 %copy.9 = bf16[256,8192]{0,1:T(8,128)(2,1)} copy(bf16[256,8192]{1,0:T(8,128)(2,1)} %param.8) | data formatting | bytes 8388608 | tf_op args[0]
  15.3 3.5 fusion.8
  18.8 3.4 fusion.10
  23.6 35.5 %all-gather.7.cloned.1.call-done = bf16[4096,512]{1,0:T(8,128)(2,1)} async-done(((bf16[256,512]{1,0:T(8,128)(2,1)}), bf16[4096,512]{1,0:T(8,128)(2,1)}) %all-gather.7.cloned.1.call-update) | async-done | bytes 4194320 | tf_op jit(solution)/shard_map/all_gather | solution.py:202
  61.9 24.9 %collective-permute-done.1 = bf16[256,2048]{0,1:T(8,128)(2,1)S(1)} collective-permute-done((bf16[256,2048]{0,1:T(8,128)(2,1)S(1)}, bf16[256,2048]{0,1:T(8,128)(2,1)S(1)}, u32[]{:S(2)}, u32[]{:S(2)}) %collective-permute-start.1) | collective-permute-done | bytes 1048608 | tf_op jit(solution)/shard_map/ppermute | solution.py:22
  87.8 33.5 %collective-permute-done.2 = bf16[256,2048]{0,1:T(8,128)(2,1)} collective-permute-done((bf16[256,2048]{0,1:T(8,128)(2,1)S(1)}, bf16[256,2048]{0,1:T(8,128)(2,1)}, u32[]{:S(2)}, u32[]{:S(2)}) %collective-permute-start.2) | collective-permute-done | bytes 1048608 | tf_op jit(solution)/shard_map/ppermute | solution.py:22
  121.3 3.2 all-gather.9.cloned.1.call-done
  124.5 11.3 %fusion.32 = bf16[1601,512]{1,0:T(8,128)(2,1)S(1)} fusion(bf16[4096,512]{1,0:T(8,128)(2,1)} %all-gather.7.cloned.1.call-done, bf16[1,1601,4096]{2,1,0:T(8,128)(2,1)} %param.9), kind=kOutput, calls=%fused_computation.21 | convolution fusion | flops 6715900416 | bytes 18949120 | tf_op jit(solution)/shard_map/dot_general | solution.py:206
  137.1 36.2 %collective-permute-done.3.refs_1_ = bf16[1601,512]{1,0:T(8,128)(2,1)S(1)} collective-permute-done((bf16[1601,512]{1,0:T(8,128)(2,1)S(1)}, bf16[1601,512]{1,0:T(8,128)(2,1)S(1)}, u32[]{:S(2)}, u32[]{:S(2)}) %collective-permute-start.3) | collective-permute-done | bytes 1639456 | tf_op jit(solution)/shard_map/ppermute | solution.py:210
  173.3 2.6 all-gather.11.cloned.1.call-done
  176.0 11.4 %fusion.29 = bf16[1601,512]{1,0:T(8,128)(2,1)S(1)} fusion(bf16[4096,512]{1,0:T(8,128)(2,1)} %all-gather.9.cloned.1.call-done, bf16[1,1601,4096]{2,1,0:T(8,128)(2,1)} %param.9), kind=kOutput, calls=%fused_computation.20 | convolution fusion | flops 6715900416 | bytes 18949120 | tf_op jit(solution)/shard_map/dot_general | solution.py:206
  190.3 34.6 %collective-permute-done.4.refs_1_ = bf16[1601,512]{1,0:T(8,128)(2,1)S(1)} collective-permute-done((bf16[1601,512]{1,0:T(8,128)(2,1)S(1)}, bf16[1601,512]{1,0:T(8,128)(2,1)S(1)}, u32[]{:S(2)}, u32[]{:S(2)}) %collective-permute-start.4) | collective-permute-done | bytes 1639456 | tf_op jit(solution)/shard_map/ppermute | solution.py:210
  227.4 11.3 %fusion.26.refs_0_ = bf16[1601,512]{1,0:T(8,128)(2,1)S(1)} fusion(bf16[4096,512]{1,0:T(8,128)(2,1)} %all-gather.11.cloned.1.call-done, bf16[1,1601,4096]{2,1,0:T(8,128)(2,1)} %param.9), kind=kOutput, calls=%fused_computation.19 | convolution fusion | flops 6715900416 | bytes 18949120 | tf_op jit(solution)/shard_map/dot_general | solution.py:206
  241.2 100.8 %collective-permute-done.5.refs_7_ = bf16[1601,512]{1,0:T(8,128)(2,1)S(1)} collective-permute-done((bf16[1601,512]{1,0:T(8,128)(2,1)S(1)}, bf16[1601,512]{1,0:T(8,128)(2,1)S(1)}, u32[]{:S(2)}, u32[]{:S(2)}) %collective-permute-start.5) | collective-permute-done | bytes 1639456 | tf_op jit(solution)/shard_map/ppermute | solution.py:27
  343.8 10.2 %fusion.23.refs_0_ = bf16[1601,512]{1,0:T(8,128)(2,1)S(1)} fusion(bf16[4096,512]{1,0:T(8,128)(2,1)S(1)} %copy-done.16, bf16[1,1601,4096]{2,1,0:T(8,128)(2,1)} %param.9), kind=kOutput, calls=%fused_computation.18 | convolution fusion | flops 6715900416 | bytes 18949120 | tf_op jit(solution)/shard_map/dot_general | solution.py:206
  356.7 24.2 %collective-permute-done.6.refs_8_ = bf16[1601,512]{1,0:T(8,128)(2,1)S(1)} collective-permute-done((bf16[1601,512]{1,0:T(8,128)(2,1)S(1)}, bf16[1601,512]{1,0:T(8,128)(2,1)S(1)}, u32[]{:S(2)}, u32[]{:S(2)}) %collective-permute-start.6) | collective-permute-done | bytes 1639456 | tf_op jit(solution)/shard_map/ppermute | solution.py:22
  382.0 11.8 %collective-permute-done.7.refs_7_ = bf16[1601,512]{1,0:T(8,128)(2,1)} collective-permute-done((bf16[1601,512]{1,0:T(8,128)(2,1)S(1)}, bf16[1601,512]{1,0:T(8,128)(2,1)}, u32[]{:S(2)}, u32[]{:S(2)}) %collective-permute-start.7) | collective-permute-done | bytes 1639456 | tf_op jit(solution)/shard_map/ppermute | solution.py:27
  400.2 3.4 broadcast_select_fusion
  404.8 4.8 convolution_convert_fusion.1
  415.5 39.4 %collective-permute-done.10.refs_4_ = bf16[256,1024]{1,0:T(8,128)(2,1)} collective-permute-done((bf16[256,1024]{1,0:T(8,128)(2,1)}, bf16[256,1024]{1,0:T(8,128)(2,1)}, u32[]{:S(2)}, u32[]{:S(2)}) %collective-permute-start.10) | collective-permute-done | bytes 524320 | tf_op jit(solution)/shard_map/ppermute | solution.py:22
  455.4 19.1 %all-gather.17.cloned.1.call-done = bf16[2048,1024]{1,0:T(8,128)(2,1)} async-done(((bf16[512,1024]{1,0:T(8,128)(2,1)}), bf16[2048,1024]{1,0:T(8,128)(2,1)}) %all-gather.17.cloned.1.call-update) | async-done | bytes 4194320 | tf_op jit(solution)/shard_map/all_gather | solution.py:202
  474.5 8.0 %convolution_convert_fusion = bf16[1024,1024]{1,0:T(8,128)(2,1)S(1)} fusion(bf16[1024,2048]{0,1:T(8,128)(2,1)} %copy-done.13, bf16[2048,1024]{1,0:T(8,128)(2,1)} %all-gather.17.cloned.1.call-done), kind=kOutput, calls=%fused_computation.22 | convolution fusion | flops 4296015872 | bytes 10485760 | tf_op jit(solution)/shard_map/dot_general | solution.py:261
  485.1 31.1 %shard_map.84 = bf16[256,1024]{1,0:T(8,128)(2,1)S(1)} custom-call(s32[5]{0:T(128)S(1)} %and_convert_fusion.refs_0_, bf16[256,1024]{1,0:T(8,128)(2,1)S(1)} %copy-done.5, bf16[256,1024]{1,0:T(8,128)(2,1)} %collective-permute-done.8.refs_2_, bf16[256,1024]{1,0:T(8,128)(2,1)} %collective-permute-done.9.refs_3_, ...), custom_call_target="tpu_custom_call" | custom-call | flops 5036310528 | bytes 8197120 | tf_op jit(solution)/shard_map/pallas_call | solution.py:126
  516.2 31.2 %shard_map.85 = bf16[256,1024]{1,0:T(8,128)(2,1)S(1)} custom-call(s32[5]{0:T(128)S(1)} %and_convert_fusion.refs_0_, bf16[256,1024]{1,0:T(8,128)(2,1)S(1)} %get-tuple-element.64.refs_1_, bf16[256,1024]{1,0:T(8,128)(2,1)S(1)} %collective-permute-done.13.refs_2_, bf16[256,1024]{1,0:T(8,128)(2,1)S(1)} %collective-permute-done.14.refs_3_, ...), custom_call_target="tpu_custom_call" | custom-call | flops 5036310528 | bytes 8197120 | tf_op jit(solution)/shard_map/pallas_call | solution.py:126
  (100 shorter events, 39.7 us)
Async XLA Ops:
  6.5 52.5 %all-gather.7.cloned.1.call-start = ((), (), s32[]{:S(2)}) async-start(), calls=%async_computation | async-start | bytes 4456448 | tf_op jit(solution)/shard_map/all_gather | solution.py:202
  8.8 115.7 %all-gather.9.cloned.1.call-start = ((), (), s32[]{:S(2)}) async-start(), calls=%async_computation.1 | async-start | bytes 4456448 | tf_op jit(solution)/shard_map/all_gather | solution.py:202
  59.1 116.8 %all-gather.11.cloned.1.call-start = ((), (), s32[]{:S(2)}) async-start(), calls=%async_computation.2 | async-start | bytes 4456448 | tf_op jit(solution)/shard_map/all_gather | solution.py:202
  59.5 27.3 %collective-permute-start.1 = (bf16[256,2048]{0,1:T(8,128)(2,1)S(1)}, bf16[256,2048]{0,1:T(8,128)(2,1)S(1)}, u32[]{:S(2)}, u32[]{:S(2)}) collective-permute-start(bf16[256,2048]{0,1:T(8,128)(2,1)S(1)} %bitcast.63), channel_id=1, source_target_pairs={{0,4},{2,6},{4,0},{6,2},{8,12},{10,14},{12,8},{14,10},{16,20},{18,... | collective-permute-start | bytes 3145736 | tf_op jit(solution)/shard_map/ppermute | solution.py:22
  60.7 60.6 %collective-permute-start.2 = (bf16[256,2048]{0,1:T(8,128)(2,1)S(1)}, bf16[256,2048]{0,1:T(8,128)(2,1)}, u32[]{:S(2)}, u32[]{:S(2)}) collective-permute-start(bf16[256,2048]{0,1:T(8,128)(2,1)S(1)} %bitcast.62), channel_id=1, source_target_pairs={{0,6},{2,4},{4,2},{6,0},{8,14},{10,12},{12,10},{14,8},{16,22},{18,... | collective-permute-start | bytes 3145736 | tf_op jit(solution)/shard_map/ppermute | solution.py:22
  124.5 102.7 %all-gather.13.cloned.1.call-start = ((), (), s32[]{:S(2)}) async-start(), calls=%async_computation.3 | async-start | bytes 4456448 | tf_op jit(solution)/shard_map/all_gather | solution.py:202
  135.8 37.5 %collective-permute-start.3 = (bf16[1601,512]{1,0:T(8,128)(2,1)S(1)}, bf16[1601,512]{1,0:T(8,128)(2,1)S(1)}, u32[]{:S(2)}, u32[]{:S(2)}) collective-permute-start(bf16[1601,512]{1,0:T(8,128)(2,1)S(1)} %fusion.32), channel_id=1, source_target_pairs={{0,1},{1,0},{2,3},{3,2},{4,5},{5,4},{6,7},{7,6},{8,9},{9,8},{10,11... | collective-permute-start | bytes 4918280 | tf_op jit(solution)/shard_map/ppermute | solution.py:210
  175.9 218.0 %all-gather.15.cloned.1.call-start = ((), (), s32[]{:S(2)}) async-start(), calls=%async_computation.4 | async-start | bytes 5242880 | tf_op jit(solution)/shard_map/all_gather | solution.py:202
  187.4 37.5 %collective-permute-start.4 = (bf16[1601,512]{1,0:T(8,128)(2,1)S(1)}, bf16[1601,512]{1,0:T(8,128)(2,1)S(1)}, u32[]{:S(2)}, u32[]{:S(2)}) collective-permute-start(bf16[1601,512]{1,0:T(8,128)(2,1)S(1)} %fusion.29), channel_id=1, source_target_pairs={{0,1},{1,0},{2,3},{3,2},{4,5},{5,4},{6,7},{7,6},{8,9},{9,8},{10,11... | collective-permute-start | bytes 4918280 | tf_op jit(solution)/shard_map/ppermute | solution.py:210
  227.2 247.3 %all-gather.17.cloned.1.call-start = ((), (), s32[]{:S(2)}) async-start(), calls=%async_computation.5 | async-start | bytes 5242880 | tf_op jit(solution)/shard_map/all_gather | solution.py:202
  239.9 102.2 %collective-permute-start.5 = (bf16[1601,512]{1,0:T(8,128)(2,1)S(1)}, bf16[1601,512]{1,0:T(8,128)(2,1)S(1)}, u32[]{:S(2)}, u32[]{:S(2)}) collective-permute-start(bf16[1601,512]{1,0:T(8,128)(2,1)S(1)} %shard_map.82.refs_6_), channel_id=1, source_target_pairs={{0,8},{2,10},{4,12},{6,14},{8,16},{10,18},{12,20},{14,22},{16,24},... | collective-permute-start | bytes 4918280 | tf_op jit(solution)/shard_map/ppermute | solution.py:27
  343.6 37.2 %collective-permute-start.6 = (bf16[1601,512]{1,0:T(8,128)(2,1)S(1)}, bf16[1601,512]{1,0:T(8,128)(2,1)S(1)}, u32[]{:S(2)}, u32[]{:S(2)}) collective-permute-start(bf16[1601,512]{1,0:T(8,128)(2,1)S(1)} %get-tuple-element.54), channel_id=1, source_target_pairs={{0,4},{2,6},{4,0},{6,2},{8,12},{10,14},{12,8},{14,10},{16,20},{18,... | collective-permute-start | bytes 4918280 | tf_op jit(solution)/shard_map/ppermute | solution.py:22
  355.2 38.7 %collective-permute-start.7 = (bf16[1601,512]{1,0:T(8,128)(2,1)S(1)}, bf16[1601,512]{1,0:T(8,128)(2,1)}, u32[]{:S(2)}, u32[]{:S(2)}) collective-permute-start(bf16[1601,512]{1,0:T(8,128)(2,1)S(1)} %shard_map.83.refs_6_), channel_id=1, source_target_pairs={{0,8},{2,10},{4,12},{6,14},{8,16},{10,18},{12,20},{14,22},{16,24},... | collective-permute-start | bytes 4918280 | tf_op jit(solution)/shard_map/ppermute | solution.py:27
  398.4 16.3 %collective-permute-start.11 = (bf16[1601,512]{1,0:T(8,128)(2,1)}, bf16[1601,512]{1,0:T(8,128)(2,1)}, u32[]{:S(2)}, u32[]{:S(2)}) collective-permute-start(bf16[1601,512]{1,0:T(8,128)(2,1)} %get-tuple-element.53), channel_id=1, source_target_pairs={{0,2},{2,0},{4,6},{6,4},{8,10},{10,8},{12,14},{14,12},{16,18},{18,... | collective-permute-start | bytes 4918280 | tf_op jit(solution)/shard_map/ppermute | solution.py:22
  403.5 51.4 %collective-permute-start.16 = (bf16[1601,512]{1,0:T(8,128)(2,1)}, bf16[1601,512]{1,0:T(8,128)(2,1)}, u32[]{:S(2)}, u32[]{:S(2)}) collective-permute-start(bf16[1601,512]{1,0:T(8,128)(2,1)} %get-tuple-element.56), channel_id=1, source_target_pairs={{0,4},{2,6},{4,0},{6,2},{8,12},{10,14},{12,8},{14,10},{16,20},{18,... | collective-permute-start | bytes 4918280 | tf_op jit(solution)/shard_map/ppermute | solution.py:22
  410.9 44.0 %collective-permute-start.10 = (bf16[256,1024]{1,0:T(8,128)(2,1)}, bf16[256,1024]{1,0:T(8,128)(2,1)}, u32[]{:S(2)}, u32[]{:S(2)}) collective-permute-start(bf16[256,1024]{1,0:T(8,128)(2,1)} %get-tuple-element.57), channel_id=1, source_target_pairs={{0,6},{2,4},{4,2},{6,0},{8,14},{10,12},{12,10},{14,8},{16,22},{18,... | collective-permute-start | bytes 1572872 | tf_op jit(solution)/shard_map/ppermute | solution.py:22
  412.7 72.0 %collective-permute-start.12 = (bf16[1601,512]{1,0:T(8,128)(2,1)}, bf16[1601,512]{1,0:T(8,128)(2,1)}, u32[]{:S(2)}, u32[]{:S(2)}) collective-permute-start(bf16[1601,512]{1,0:T(8,128)(2,1)} %copy-done.17), channel_id=1, source_target_pairs={{0,2},{2,0},{4,6},{6,4},{8,10},{10,8},{12,14},{14,12},{16,18},{18,... | collective-permute-start | bytes 4918280 | tf_op jit(solution)/shard_map/ppermute | solution.py:22
  413.5 69.4 %collective-permute-start.9 = (bf16[256,1024]{1,0:T(8,128)(2,1)}, bf16[256,1024]{1,0:T(8,128)(2,1)}, u32[]{:S(2)}, u32[]{:S(2)}) collective-permute-start(bf16[256,1024]{1,0:T(8,128)(2,1)} %get-tuple-element.58), channel_id=1, source_target_pairs={{0,4},{2,6},{4,0},{6,2},{8,12},{10,14},{12,8},{14,10},{16,20},{18,... | collective-permute-start | bytes 1572872 | tf_op jit(solution)/shard_map/ppermute | solution.py:22
  414.7 68.6 %collective-permute-start.8 = (bf16[256,1024]{1,0:T(8,128)(2,1)}, bf16[256,1024]{1,0:T(8,128)(2,1)}, u32[]{:S(2)}, u32[]{:S(2)}) collective-permute-start(bf16[256,1024]{1,0:T(8,128)(2,1)} %get-tuple-element.59), channel_id=1, source_target_pairs={{0,2},{2,0},{4,6},{6,4},{8,10},{10,8},{12,14},{14,12},{16,18},{18,... | collective-permute-start | bytes 1572872 | tf_op jit(solution)/shard_map/ppermute | solution.py:22
  454.9 61.3 %collective-permute-start.17 = (bf16[1601,512]{1,0:T(8,128)(2,1)}, bf16[1601,512]{1,0:T(8,128)(2,1)}, u32[]{:S(2)}, u32[]{:S(2)}) collective-permute-start(bf16[1601,512]{1,0:T(8,128)(2,1)} %get-tuple-element.55), channel_id=1, source_target_pairs={{0,2},{2,0},{4,6},{6,4},{8,10},{10,8},{12,14},{14,12},{16,18},{18,... | collective-permute-start | bytes 4918280 | tf_op jit(solution)/shard_map/ppermute | solution.py:22
  454.9 61.3 %collective-permute-start.18 = (bf16[1601,512]{1,0:T(8,128)(2,1)}, bf16[1601,512]{1,0:T(8,128)(2,1)}, u32[]{:S(2)}, u32[]{:S(2)}) collective-permute-start(bf16[1601,512]{1,0:T(8,128)(2,1)} %collective-permute-done.16.refs_8_), channel_id=1, source_target_pairs={{0,2},{2,0},{4,6},{6,4},{8,10},{10,8},{12,14},{14,12},{16,18},{18,... | collective-permute-start | bytes 4918280 | tf_op jit(solution)/shard_map/ppermute | solution.py:22
  482.8 33.4 %collective-permute-start.15 = (bf16[256,1024]{1,0:T(8,128)(2,1)S(1)}, bf16[256,1024]{1,0:T(8,128)(2,1)S(1)}, u32[]{:S(2)}, u32[]{:S(2)}) collective-permute-start(bf16[256,1024]{1,0:T(8,128)(2,1)S(1)} %get-tuple-element.61), channel_id=1, source_target_pairs={{0,6},{2,4},{4,2},{6,0},{8,14},{10,12},{12,10},{14,8},{16,22},{18,... | collective-permute-start | bytes 1572872 | tf_op jit(solution)/shard_map/ppermute | solution.py:22
  483.3 32.9 %collective-permute-start.14 = (bf16[256,1024]{1,0:T(8,128)(2,1)S(1)}, bf16[256,1024]{1,0:T(8,128)(2,1)S(1)}, u32[]{:S(2)}, u32[]{:S(2)}) collective-permute-start(bf16[256,1024]{1,0:T(8,128)(2,1)S(1)} %get-tuple-element.62), channel_id=1, source_target_pairs={{0,4},{2,6},{4,0},{6,2},{8,12},{10,14},{12,8},{14,10},{16,20},{18,... | collective-permute-start | bytes 1572872 | tf_op jit(solution)/shard_map/ppermute | solution.py:22
  484.7 31.5 %collective-permute-start.13 = (bf16[256,1024]{1,0:T(8,128)(2,1)S(1)}, bf16[256,1024]{1,0:T(8,128)(2,1)S(1)}, u32[]{:S(2)}, u32[]{:S(2)}) collective-permute-start(bf16[256,1024]{1,0:T(8,128)(2,1)S(1)} %get-tuple-element.63), channel_id=1, source_target_pairs={{0,2},{2,0},{4,6},{6,4},{8,10},{10,8},{12,14},{14,12},{16,18},{18,... | collective-permute-start | bytes 1572872 | tf_op jit(solution)/shard_map/ppermute | solution.py:22
  (19 other events, 618.7 us)
Sparse Core Ops, SparseCore 0:
  9.5 49.5 all-gather.6
  61.2 63.1 all-gather.8
  126.6 49.2 all-gather.10
  177.9 49.2 all-gather.12
  228.6 108.8 all-gather.14
  394.0 80.4 all-gather.16
